TPU v7x, 32 devices: a whole 2x2x4 slice. The times are simulated.
32 devices in a mesh: blk: 8 (over z, x), win: 4 (over y, core).
Axes of the slice: x: 2, y: 2, z: 4, core: 2. Of those that a mesh axis runs over, the one named last changes fastest.
Arguments:
- samples: bfloat16 [1024, 32, 2048], P('blk', 'win'), may hold values from -6 to 6
- pair_offsets: int32 [24], P('blk'), may hold values from 0 to 4, as said below
- pair_count: int32 [8], P('blk'), may hold values from 1 to 3
Outputs:
- cross_spectra: bfloat16 [24, 128, 2, 128, 128], P('blk', 'win')
Inputs may be any that keep to these rules, and one draw needn't show every extreme that they name: `pair_offsets`: entry w * 3 + s belongs to worker w. The live slots of a worker (s below its count) hold different offsets, with w + offset below the number of blocks; the other slots hold 0.
All inputs are finite; a program needn't handle non-finite values.
Results may differ from a plain program's by a relative error of at most 0.0068.
Values may be sent and summed in bfloat16 or wider, within the bound.
A program may use at most 64 MiB of HBM per device.

v0:
```python
import math
import jax
import jax.numpy as jnp
from jax import lax
from jax.sharding import PartitionSpec as P

BINS = 128
BIN0 = 32
SMOOTH = 4
OFFSET = 4
water_level = 0.1
epsilon = 1e-06


def shifted(block, axis, distance):
    devices = range(lax.axis_size(axis))
    route = [(i - distance, i) for i in devices if i - distance in devices]
    return lax.ppermute(block, axis, route)


def dft_table(length):
    sample_idx = jnp.arange(length, dtype=jnp.int32)
    bin_freqs = BIN0 + jnp.arange(BINS, dtype=jnp.int32)
    phases = sample_idx[:, None] * bin_freqs[None, :] % length
    angles = phases.astype(jnp.float32) * (2.0 * math.pi / length)
    window_taper = 0.5 - 0.5 * jnp.cos(
        (sample_idx.astype(jnp.float32) + 0.5) * (2.0 * math.pi / length)
    )
    cosines = window_taper[:, None] * jnp.cos(angles)
    sines = -window_taper[:, None] * jnp.sin(angles)
    return jnp.concatenate([cosines, sines], axis=1).astype(jnp.bfloat16)


def band_weights():
    bin_index = jnp.arange(BINS, dtype=jnp.int32)
    inside = (jnp.abs(bin_index[:, None] - bin_index[None, :]) <= SMOOTH).astype(jnp.float32)
    return inside / jnp.sum(inside, axis=0, keepdims=True)


def whiten_spectrum(spectrum, weights):
    energy = spectrum[:, 0] * spectrum[:, 0] + spectrum[:, 1] * spectrum[:, 1]
    smoothed = jnp.einsum("wjc,jb->wbc", energy, weights, precision=lax.Precision.HIGHEST)
    average = jnp.mean(energy, axis=1, keepdims=True)
    factor = lax.rsqrt(smoothed + water_level * average + epsilon)
    return (spectrum * factor[:, None]).astype(jnp.bfloat16)


def cross_pair(left_side, partner, windows):
    right_side = partner.reshape(2 * windows, partner.shape[2], partner.shape[3])
    product = lax.dot_general(
        left_side, right_side, (((1,), (0,)), ((2,), (1,))), preferred_element_type=jnp.float32
    )
    return product * (1.0 / windows)


def shards(samples, pair_offsets, pair_count):
    channels, win_dev, length = samples.shape
    table = dft_table(length)
    weights = band_weights()
    spectrum = jnp.einsum("cwt,tk->wkc", samples, table, preferred_element_type=jnp.float32)
    whitened = whiten_spectrum(spectrum.reshape(win_dev, 2, BINS, channels), weights)
    by_bins = lax.all_to_all(whitened, "win", split_axis=2, concat_axis=0, tiled=True)
    windows = by_bins.shape[0]
    bins_dev = by_bins.shape[2]
    swapped = jnp.stack([by_bins[:, 1], -by_bins[:, 0]], axis=1)
    left_side = jnp.stack([by_bins, swapped], axis=0).reshape(2, 2 * windows, bins_dev, channels)
    neighbours = [by_bins]
    for distance in range(1, OFFSET + 1):
        neighbours.append(shifted(by_bins, "blk", -distance))
    nearby = jnp.stack(neighbours, axis=0)
    live_count = pair_count[0]
    slot_total = pair_offsets.shape[0]
    results = []
    for slot_rank in range(slot_total):
        partner = lax.dynamic_index_in_dim(nearby, pair_offsets[slot_rank], 0, keepdims=False)
        value = cross_pair(left_side, partner, windows)
        results.append(
            jnp.where(slot_rank < live_count, value, jnp.zeros_like(value)).astype(jnp.bfloat16)
        )
    cross_spectra = jnp.stack(results, axis=0)
    return cross_spectra


def solution(mesh):
    in_specs = (P("blk", "win", None), P("blk"), P("blk"))
    out_specs = P("blk", "win", None, None, None)
    return jax.shard_map(shards, mesh=mesh, in_specs=in_specs, out_specs=out_specs, check_vma=False)
```

profile of v0, /device:TPU:0, one launch (start us, length us, event | category | flops | bytes accessed | tf_op | source)
XLA Modules:
  0.0 109.8 jit_solution(9315533526000073080)
XLA Ops:
  0.0 0.1 convert_reduce_fusion
  0.1 0.1 multiply_subtract_fusion
  0.2 4.5 %multiply_convert_fusion.2 = (bf16[2048,128]{0,1:T(8,128)(2,1)S(1)}, bf16[2048,128]{0,1:T(8,128)(2,1)S(1)}) fusion(s32[128]{0:T(128)S(1)} %iota_add_fusion, f32[2048]{0:T(1024)S(1)} %get-tuple-element.15, f32[2048]{0:T(1024)S(1)} %get-tuple-element.16), kind=kLoop, calls=%fused_computation.25 | loop fusion | flops 4718592 | bytes 1065472 | tf_op jit(solution)/shard_map/convert
  4.7 7.1 %fusion = f32[256,128,8]{1,0,2:T(8,128)S(1)} fusion(bf16[128,8,2048]{2,1,0:T(8,128)(2,1)} %param.3, bf16[2048,128]{0,1:T(8,128)(2,1)S(1)} %get-tuple-element.14, bf16[2048,128]{0,1:T(8,128)(2,1)S(1)} %get-tuple-element.13), kind=kOutput, calls=%fused_computation.1 | convolution fusion | flops 1075838976 | bytes 6291456 | tf_op jit(solution)/shard_map/cwt,tk->wkc/dot_general | solution.py:60
  11.9 0.1 fusion.18
  12.0 0.0 copy-start
  12.0 0.6 fusion.7
  12.7 0.1 multiply_convert_fusion
  12.8 1.3 %copy.15 = bf16[8,2,128,128]{3,1,0,2:T(2,128)(2,1)} copy(bf16[8,2,128,128]{3,2,1,0:T(8,128)(2,1)S(1)} %multiply_convert_fusion) | data formatting | bytes 1048576 | tf_op jit(solution)/shard_map/convert_element_type | solution.py:45
  14.1 4.2 %all-to-all-start = ((bf16[8,2,128,128]{3,1,0,2:T(2,128)(2,1)}), bf16[8,2,128,128]{3,1,0,2:T(2,128)(2,1)S(1)}, u32[]{:S(2)}, u32[]{:S(2)}) async-start(bf16[8,2,128,128]{3,1,0,2:T(2,128)(2,1)} %copy.15), calls=%async_computation | async-start | bytes 1048576 | tf_op jit(solution)/shard_map/all_to_all | solution.py:62
  18.3 0.7 fusion.31
  25.2 1.9 %all-to-all-done = bf16[8,2,128,128]{3,1,0,2:T(2,128)(2,1)S(1)} async-done(((bf16[8,2,128,128]{3,1,0,2:T(2,128)(2,1)}), bf16[8,2,128,128]{3,1,0,2:T(2,128)(2,1)S(1)}, u32[]{:S(2)}, u32[]{:S(2)}) %all-to-all-start) | async-done | bytes 524320 | tf_op jit(solution)/shard_map/all_to_all | solution.py:62
  27.2 0.5 copy.16
  27.7 1.3 %collective-permute-start.2 = (bf16[32,2,32,128]{3,1,0,2:T(2,128)(2,1)S(1)}, bf16[32,2,32,128]{3,1,0,2:T(2,128)(2,1)S(1)}, u32[]{:S(2)}, u32[]{:S(2)}) collective-permute-start(bf16[32,2,32,128]{3,1,0,2:T(2,128)(2,1)S(1)} %bitcast.62), channel_id=1, source_target_pairs={{12,0},{16,4},{20,8},{24,12},{28,16},{13,1},{17,5},{21,9},{25,13},... | collective-permute-start | bytes 1572872 | tf_op jit(solution)/shard_map/ppermute | solution.py:18
  29.0 1.3 %collective-permute-start.1 = (bf16[32,2,32,128]{3,1,0,2:T(2,128)(2,1)S(1)}, bf16[32,2,32,128]{3,1,0,2:T(2,128)(2,1)S(1)}, u32[]{:S(2)}, u32[]{:S(2)}) collective-permute-start(bf16[32,2,32,128]{3,1,0,2:T(2,128)(2,1)S(1)} %bitcast.63), channel_id=1, source_target_pairs={{8,0},{12,4},{16,8},{20,12},{24,16},{28,20},{9,1},{13,5},{17,9},{2... | collective-permute-start | bytes 1572872 | tf_op jit(solution)/shard_map/ppermute | solution.py:18
  30.3 1.3 %collective-permute-start = (bf16[32,2,32,128]{3,1,0,2:T(2,128)(2,1)S(1)}, bf16[32,2,32,128]{3,1,0,2:T(2,128)(2,1)S(1)}, u32[]{:S(2)}, u32[]{:S(2)}) collective-permute-start(bf16[32,2,32,128]{3,1,0,2:T(2,128)(2,1)S(1)} %bitcast.64), channel_id=1, source_target_pairs={{4,0},{8,4},{12,8},{16,12},{20,16},{24,20},{28,24},{5,1},{9,5},{13... | collective-permute-start | bytes 1572872 | tf_op jit(solution)/shard_map/ppermute | solution.py:18
  31.6 1.5 %collective-permute-start.3 = (bf16[32,2,32,128]{3,1,0,2:T(2,128)(2,1)S(1)}, bf16[32,2,32,128]{3,1,0,2:T(2,128)(2,1)S(1)}, u32[]{:S(2)}, u32[]{:S(2)}) collective-permute-start(bf16[32,2,32,128]{3,1,0,2:T(2,128)(2,1)S(1)} %bitcast.65), channel_id=1, source_target_pairs={{16,0},{20,4},{24,8},{28,12},{17,1},{21,5},{25,9},{29,13},{18,2},{... | collective-permute-start | bytes 1572872 | tf_op jit(solution)/shard_map/ppermute | solution.py:18
  33.1 0.9 fusion.30
  34.1 0.4 constant_dynamic-update-slice_fusion
  34.5 1.2 %pad_maximum_fusion.2 = bf16[32,2,32,128]{3,1,0,2:T(2,128)(2,1)S(1)} fusion(bf16[32,1,32,128]{3,1,0,2:T(2,128)(2,1)S(1)} %get-tuple-element.9, bf16[32,1,32,128]{3,1,0,2:T(2,128)(2,1)S(1)} %get-tuple-element.8), kind=kLoop, calls=%fused_computation.33 | loop fusion | flops 1048576 | bytes 1048576 | tf_op jit(solution)/shard_map/stack | solution.py:65
  35.7 20.0 %collective-permute-done = bf16[32,2,32,128]{3,1,0,2:T(2,128)(2,1)S(1)} collective-permute-done((bf16[32,2,32,128]{3,1,0,2:T(2,128)(2,1)S(1)}, bf16[32,2,32,128]{3,1,0,2:T(2,128)(2,1)S(1)}, u32[]{:S(2)}, u32[]{:S(2)}) %collective-permute-start) | collective-permute-done | bytes 524320 | tf_op jit(solution)/shard_map/ppermute | solution.py:18
  55.7 0.5 bitcast_dynamic-update-slice_fusion.3
  56.2 0.0 collective-permute-done.1
  56.3 0.5 bitcast_dynamic-update-slice_fusion.2
  56.8 0.5 bitcast_dynamic-update-slice_fusion.1
  57.3 44.6 %collective-permute-done.3 = bf16[32,2,32,128]{3,1,0,2:T(2,128)(2,1)S(1)} collective-permute-done((bf16[32,2,32,128]{3,1,0,2:T(2,128)(2,1)S(1)}, bf16[32,2,32,128]{3,1,0,2:T(2,128)(2,1)S(1)}, u32[]{:S(2)}, u32[]{:S(2)}) %collective-permute-start.3) | collective-permute-done | bytes 524320 | tf_op jit(solution)/shard_map/ppermute | solution.py:18
  101.8 0.5 bitcast_dynamic-update-slice_fusion
  102.3 1.5 %constant_dynamic-slice_fusion.2 = (bf16[1,32,2,32,128]{4,2,1,3,0:T(2,128)(2,1)S(1)}, bf16[1,32,2,32,128]{4,2,1,3,0:T(2,128)(2,1)S(1)}, bf16[1,32,2,32,128]{4,2,1,3,0:T(2,128)(2,1)S(1)}) fusion(bf16[5,32,2,32,128]{4,2,1,3,0:T(2,128)(2,1)S(1)} %bitcast_dynamic-update-slice_fusion, s32[]{:T(128)S(6)} %select_n.41, s32[]{:T(128)S(6)} %select_n.47, s32[]{:T(128)S(6)} %select_n.44), kind=kLoop, calls=%fused_computation.52 | loop fusion | bytes 3145740 | tf_op jit(solution)/shard_map/jit(dynamic_index_in_dim)/dynamic_slice | solution.py:75
  103.8 0.9 fusion.4
  104.7 0.9 fusion.2
  105.7 0.9 fusion.3
  106.6 3.2 %pad_maximum_fusion = bf16[3,32,2,128,128]{4,3,2,1,0:T(8,128)(2,1)} fusion(bf16[1,32,2,128,128]{4,3,2,1,0:T(8,128)(2,1)S(1)} %fusion.4, bf16[1,32,2,128,128]{4,3,2,1,0:T(8,128)(2,1)S(1)} %fusion.3, bf16[1,32,2,128,128]{4,3,2,1,0:T(8,128)(2,1)S(1)} %fusion.2), kind=kLoop, calls=%fused_computation | loop fusion | flops 6291456 | bytes 12582912 | tf_op jit(solution)/shard_map/stack | solution.py:80
  (4 shorter events, 0.0 us)
Async XLA Ops:
  12.0 6.4 %copy-start = (s32[3]{0:T(128)S(1)}, s32[3]{0:T(128)}, u32[]{:S(2)}) copy-start(s32[3]{0:T(128)} %param.4) | copy-start | bytes 40
  14.1 13.1 %all-to-all-start = ((bf16[8,2,128,128]{3,1,0,2:T(2,128)(2,1)}), bf16[8,2,128,128]{3,1,0,2:T(2,128)(2,1)S(1)}, u32[]{:S(2)}, u32[]{:S(2)}) async-start(bf16[8,2,128,128]{3,1,0,2:T(2,128)(2,1)} %copy.15), calls=%async_computation | async-start | bytes 1048576 | tf_op jit(solution)/shard_map/all_to_all | solution.py:62
  27.7 29.0 %collective-permute-start.2 = (bf16[32,2,32,128]{3,1,0,2:T(2,128)(2,1)S(1)}, bf16[32,2,32,128]{3,1,0,2:T(2,128)(2,1)S(1)}, u32[]{:S(2)}, u32[]{:S(2)}) collective-permute-start(bf16[32,2,32,128]{3,1,0,2:T(2,128)(2,1)S(1)} %bitcast.62), channel_id=1, source_target_pairs={{12,0},{16,4},{20,8},{24,12},{28,16},{13,1},{17,5},{21,9},{25,13},... | collective-permute-start | bytes 1572872 | tf_op jit(solution)/shard_map/ppermute | solution.py:18
  29.0 27.2 %collective-permute-start.1 = (bf16[32,2,32,128]{3,1,0,2:T(2,128)(2,1)S(1)}, bf16[32,2,32,128]{3,1,0,2:T(2,128)(2,1)S(1)}, u32[]{:S(2)}, u32[]{:S(2)}) collective-permute-start(bf16[32,2,32,128]{3,1,0,2:T(2,128)(2,1)S(1)} %bitcast.63), channel_id=1, source_target_pairs={{8,0},{12,4},{16,8},{20,12},{24,16},{28,20},{9,1},{13,5},{17,9},{2... | collective-permute-start | bytes 1572872 | tf_op jit(solution)/shard_map/ppermute | solution.py:18
  30.3 25.4 %collective-permute-start = (bf16[32,2,32,128]{3,1,0,2:T(2,128)(2,1)S(1)}, bf16[32,2,32,128]{3,1,0,2:T(2,128)(2,1)S(1)}, u32[]{:S(2)}, u32[]{:S(2)}) collective-permute-start(bf16[32,2,32,128]{3,1,0,2:T(2,128)(2,1)S(1)} %bitcast.64), channel_id=1, source_target_pairs={{4,0},{8,4},{12,8},{16,12},{20,16},{24,20},{28,24},{5,1},{9,5},{13... | collective-permute-start | bytes 1572872 | tf_op jit(solution)/shard_map/ppermute | solution.py:18
  31.6 70.2 %collective-permute-start.3 = (bf16[32,2,32,128]{3,1,0,2:T(2,128)(2,1)S(1)}, bf16[32,2,32,128]{3,1,0,2:T(2,128)(2,1)S(1)}, u32[]{:S(2)}, u32[]{:S(2)}) collective-permute-start(bf16[32,2,32,128]{3,1,0,2:T(2,128)(2,1)S(1)} %bitcast.65), channel_id=1, source_target_pairs={{16,0},{20,4},{24,8},{28,12},{17,1},{21,5},{25,9},{29,13},{18,2},{... | collective-permute-start | bytes 1572872 | tf_op jit(solution)/shard_map/ppermute | solution.py:18
where the time goes:
time: 110 us
  waiting for transfers between devices  66.6 us (61%)
  matrix products  10.6 us (10%)
  other arithmetic  10.2 us (9%)
  starting transfers between devices  9.58 us (9%)
  between operations  6.46 us (6%)
  local copies, waits for them, and re-layouts  6.39 us (6%)
    ppermute x4, waiting for transfers between devices, shifted(): return lax.ppermute(block, axis, route)  64.6 us
    dot_general x1, matrix products, shards(): jnp.einsum('cwt,tk->wkc', samples, table, preferred_element_type=jnp.floa...  7.15 us
    ppermute x4, starting transfers between devices, shifted(): return lax.ppermute(block, axis, route)  5.35 us
    another operation x1, other arithmetic  4.53 us
    all_to_all x1, starting transfers between devices, shards(): lax.all_to_all(whitened, 'win', split_axis=2, concat_axis=0, tiled=True)  4.24 us
    another operation x1, other arithmetic, shards(): cross_spectra = jnp.stack(results, axis=0)  3.15 us
    dot_general x3, matrix products, cross_pair(): lax.dot_general(left_side, right_side, (((1,), (0,)), ((2,), (1,))), pref...  2.8 us
  transfers between devices with their start and end apart: 5, of which 3 were waited for; matrix products, arithmetic and copies ran while one was open for 4% of the time, Pallas kernels for 0%

commit v1 on v0

--- a/solution.py
+++ b/solution.py
@@ -59,7 +59,10 @@
     weights = band_weights()
     spectrum = jnp.einsum("cwt,tk->wkc", samples, table, preferred_element_type=jnp.float32)
     whitened = whiten_spectrum(spectrum.reshape(win_dev, 2, BINS, channels), weights)
-    by_bins = lax.all_to_all(whitened, "win", split_axis=2, concat_axis=0, tiled=True)
+    by_bins = jnp.concatenate(
+        lax.all_to_all(jnp.stack(jnp.split(whitened, lax.axis_size("win"), axis=2)), "win", 0, 0),
+        axis=0,
+    )
     windows = by_bins.shape[0]
     bins_dev = by_bins.shape[2]
     swapped = jnp.stack([by_bins[:, 1], -by_bins[:, 0]], axis=1)

time: 110 us -> 110 us (level)
    convert_element_type x1 -> x0, local copies, waits for them, and re-layouts: 1.33 us -> none  [whiten_spectrum(): return (spectrum * factor[:, None]).astype(jnp.bfloat16)]
    another operation x1 -> x2, other arithmetic: 4.53 us -> 5.4 us
  transfers between devices with their start and end apart: 5 -> 5, of which waited for: 3 -> 3; matrix products, arithmetic and copies ran while one was open for 4% -> 5% of each run, Pallas kernels for 0% -> 0%
where the time goes in v1:
time: 110 us; the launch traced here: 109 us
  waiting for transfers between devices  65.7 us (60%)
  other arithmetic  11.1 us (10%)
  matrix products  10.6 us (10%)
  starting transfers between devices  9.58 us (9%)
  between operations  6.7 us (6%)
  local copies, waits for them, and re-layouts  5.76 us (5%)
    ppermute x4, waiting for transfers between devices, shifted(): return lax.ppermute(block, axis, route)  63.9 us
    dot_general x1, matrix products, shards(): jnp.einsum('cwt,tk->wkc', samples, table, preferred_element_type=jnp.floa...  7.15 us
    ppermute x4, starting transfers between devices, shifted(): return lax.ppermute(block, axis, route)  5.35 us
    another operation x1, other arithmetic  4.53 us
    all_to_all x1, starting transfers between devices, shards(): lax.all_to_all(jnp.stack(jnp.split(whitened, lax.axis_size('win'), axis=2...  4.24 us
    another operation x1, other arithmetic, shards(): cross_spectra = jnp.stack(results, axis=0)  3.15 us
    dot_general x3, matrix products, cross_pair(): lax.dot_general(left_side, right_side, (((1,), (0,)), ((2,), (1,))), pref...  2.82 us
  transfers between devices with their start and end apart: 5, of which 3 were waited for; matrix products, arithmetic and copies ran while one was open for 5% of the time, Pallas kernels for 0%

profile of v1, /device:TPU:0, one launch (start us, length us, event | category | flops | bytes accessed | tf_op | source)
XLA Modules:
  0.0 109.4 jit_solution(18362155260087869472)
XLA Ops:
  0.0 0.1 convert_reduce_fusion
  0.1 0.1 multiply_subtract_fusion
  0.2 4.5 %multiply_convert_fusion.2 = (bf16[2048,128]{0,1:T(8,128)(2,1)S(1)}, bf16[2048,128]{0,1:T(8,128)(2,1)S(1)}) fusion(s32[128]{0:T(128)S(1)} %iota_add_fusion, f32[2048]{0:T(1024)S(1)} %get-tuple-element.19, f32[2048]{0:T(1024)S(1)} %get-tuple-element.20), kind=kLoop, calls=%fused_computation.25 | loop fusion | flops 4718592 | bytes 1065472 | tf_op jit(solution)/shard_map/convert
  4.7 7.1 %fusion = f32[256,128,8]{1,0,2:T(8,128)S(1)} fusion(bf16[128,8,2048]{2,1,0:T(8,128)(2,1)} %param.3, bf16[2048,128]{0,1:T(8,128)(2,1)S(1)} %get-tuple-element.18, bf16[2048,128]{0,1:T(8,128)(2,1)S(1)} %get-tuple-element.17), kind=kOutput, calls=%fused_computation.1 | convolution fusion | flops 1075838976 | bytes 6291456 | tf_op jit(solution)/shard_map/cwt,tk->wkc/dot_general | solution.py:60
  11.9 0.1 fusion.20
  12.0 0.6 fusion.7
  12.6 0.1 multiply_convert_fusion
  12.8 0.1 slice_bitcast_fusion.5
  12.8 0.9 pad_maximum_fusion.2
  13.7 4.2 %all-to-all-start = ((bf16[4,8,2,32,128]{4,3,2,1,0:T(8,128)(2,1)}), bf16[4,8,2,32,128]{4,3,2,1,0:T(8,128)(2,1)S(1)}, u32[]{:S(2)}, u32[]{:S(2)}) async-start(bf16[4,8,2,32,128]{4,3,2,1,0:T(8,128)(2,1)} %pad_maximum_fusion.2), calls=%async_computation | async-start | bytes 1048576 | tf_op jit(solution)/shard_map/all_to_all | solution.py:63
  17.9 0.6 fusion.33
  25.0 1.7 %all-to-all-done = bf16[4,8,2,32,128]{4,3,2,1,0:T(8,128)(2,1)S(1)} async-done(((bf16[4,8,2,32,128]{4,3,2,1,0:T(8,128)(2,1)}), bf16[4,8,2,32,128]{4,3,2,1,0:T(8,128)(2,1)S(1)}, u32[]{:S(2)}, u32[]{:S(2)}) %all-to-all-start) | async-done | bytes 524320 | tf_op jit(solution)/shard_map/all_to_all | solution.py:63
  26.8 0.5 copy.8
  27.3 1.3 %collective-permute-start.2 = (bf16[32,2,32,128]{3,1,0,2:T(2,128)(2,1)S(1)}, bf16[32,2,32,128]{3,1,0,2:T(2,128)(2,1)S(1)}, u32[]{:S(2)}, u32[]{:S(2)}) collective-permute-start(bf16[32,2,32,128]{3,1,0,2:T(2,128)(2,1)S(1)} %copy.8), channel_id=1, source_target_pairs={{12,0},{16,4},{20,8},{24,12},{28,16},{13,1},{17,5},{21,9},{25,13},... | collective-permute-start | bytes 1572872 | tf_op jit(solution)/shard_map/ppermute | solution.py:18
  28.6 1.3 %collective-permute-start.1 = (bf16[32,2,32,128]{3,1,0,2:T(2,128)(2,1)S(1)}, bf16[32,2,32,128]{3,1,0,2:T(2,128)(2,1)S(1)}, u32[]{:S(2)}, u32[]{:S(2)}) collective-permute-start(bf16[32,2,32,128]{3,1,0,2:T(2,128)(2,1)S(1)} %copy.8), channel_id=1, source_target_pairs={{8,0},{12,4},{16,8},{20,12},{24,16},{28,20},{9,1},{13,5},{17,9},{2... | collective-permute-start | bytes 1572872 | tf_op jit(solution)/shard_map/ppermute | solution.py:18
  29.9 1.3 %collective-permute-start = (bf16[32,2,32,128]{3,1,0,2:T(2,128)(2,1)S(1)}, bf16[32,2,32,128]{3,1,0,2:T(2,128)(2,1)S(1)}, u32[]{:S(2)}, u32[]{:S(2)}) collective-permute-start(bf16[32,2,32,128]{3,1,0,2:T(2,128)(2,1)S(1)} %copy.8), channel_id=1, source_target_pairs={{4,0},{8,4},{12,8},{16,12},{20,16},{24,20},{28,24},{5,1},{9,5},{13... | collective-permute-start | bytes 1572872 | tf_op jit(solution)/shard_map/ppermute | solution.py:18
  31.2 1.5 %collective-permute-start.3 = (bf16[32,2,32,128]{3,1,0,2:T(2,128)(2,1)S(1)}, bf16[32,2,32,128]{3,1,0,2:T(2,128)(2,1)S(1)}, u32[]{:S(2)}, u32[]{:S(2)}) collective-permute-start(bf16[32,2,32,128]{3,1,0,2:T(2,128)(2,1)S(1)} %copy.8), channel_id=1, source_target_pairs={{16,0},{20,4},{24,8},{28,12},{17,1},{21,5},{25,9},{29,13},{18,2},{... | collective-permute-start | bytes 1572872 | tf_op jit(solution)/shard_map/ppermute | solution.py:18
  32.7 0.9 fusion.32
  33.7 0.5 copy_dynamic-update-slice_fusion
  34.2 1.2 %pad_maximum_fusion.3 = bf16[32,2,32,128]{3,1,0,2:T(2,128)(2,1)S(1)} fusion(bf16[32,1,32,128]{3,1,0,2:T(2,128)(2,1)S(1)} %get-tuple-element.9, bf16[32,1,32,128]{3,1,0,2:T(2,128)(2,1)S(1)} %get-tuple-element.8), kind=kLoop, calls=%fused_computation.36 | loop fusion | flops 1048576 | bytes 1048576 | tf_op jit(solution)/shard_map/stack | solution.py:68
  35.4 0.5 copy.7
  36.0 19.4 %collective-permute-done = bf16[32,2,32,128]{3,1,0,2:T(2,128)(2,1)S(1)} collective-permute-done((bf16[32,2,32,128]{3,1,0,2:T(2,128)(2,1)S(1)}, bf16[32,2,32,128]{3,1,0,2:T(2,128)(2,1)S(1)}, u32[]{:S(2)}, u32[]{:S(2)}) %collective-permute-start) | collective-permute-done | bytes 524320 | tf_op jit(solution)/shard_map/ppermute | solution.py:18
  55.3 0.5 bitcast_dynamic-update-slice_fusion.3
  55.9 0.5 bitcast_dynamic-update-slice_fusion.2
  56.4 0.5 bitcast_dynamic-update-slice_fusion.1
  56.9 44.6 %collective-permute-done.3 = bf16[32,2,32,128]{3,1,0,2:T(2,128)(2,1)S(1)} collective-permute-done((bf16[32,2,32,128]{3,1,0,2:T(2,128)(2,1)S(1)}, bf16[32,2,32,128]{3,1,0,2:T(2,128)(2,1)S(1)}, u32[]{:S(2)}, u32[]{:S(2)}) %collective-permute-start.3) | collective-permute-done | bytes 524320 | tf_op jit(solution)/shard_map/ppermute | solution.py:18
  101.4 0.5 bitcast_dynamic-update-slice_fusion
  101.9 1.5 %constant_dynamic-slice_fusion.2 = (bf16[1,32,2,32,128]{4,2,1,3,0:T(2,128)(2,1)S(1)}, bf16[1,32,2,32,128]{4,2,1,3,0:T(2,128)(2,1)S(1)}, bf16[1,32,2,32,128]{4,2,1,3,0:T(2,128)(2,1)S(1)}) fusion(bf16[5,32,2,32,128]{4,2,1,3,0:T(2,128)(2,1)S(1)} %bitcast_dynamic-update-slice_fusion, s32[]{:T(128)S(6)} %select_n.41, s32[]{:T(128)S(6)} %select_n.47, s32[]{:T(128)S(6)} %select_n.44), kind=kLoop, calls=%fused_computation.59 | loop fusion | bytes 3145740 | tf_op jit(solution)/shard_map/jit(dynamic_index_in_dim)/dynamic_slice | solution.py:78
  103.4 0.9 fusion.4
  104.3 0.9 fusion.2
  105.3 0.9 fusion.3
  106.2 3.2 %pad_maximum_fusion = bf16[3,32,2,128,128]{4,3,2,1,0:T(8,128)(2,1)} fusion(bf16[1,32,2,128,128]{4,3,2,1,0:T(8,128)(2,1)S(1)} %fusion.4, bf16[1,32,2,128,128]{4,3,2,1,0:T(8,128)(2,1)S(1)} %fusion.3, bf16[1,32,2,128,128]{4,3,2,1,0:T(8,128)(2,1)S(1)} %fusion.2), kind=kLoop, calls=%fused_computation | loop fusion | flops 6291456 | bytes 12582912 | tf_op jit(solution)/shard_map/stack | solution.py:83
  (6 shorter events, 0.0 us)
Async XLA Ops:
  12.6 5.3 %copy-start = (s32[3]{0:T(128)S(1)}, s32[3]{0:T(128)}, u32[]{:S(2)}) copy-start(s32[3]{0:T(128)} %param.4) | copy-start | bytes 40
  13.7 13.1 %all-to-all-start = ((bf16[4,8,2,32,128]{4,3,2,1,0:T(8,128)(2,1)}), bf16[4,8,2,32,128]{4,3,2,1,0:T(8,128)(2,1)S(1)}, u32[]{:S(2)}, u32[]{:S(2)}) async-start(bf16[4,8,2,32,128]{4,3,2,1,0:T(8,128)(2,1)} %pad_maximum_fusion.2), calls=%async_computation | async-start | bytes 1048576 | tf_op jit(solution)/shard_map/all_to_all | solution.py:63
  27.3 29.0 %collective-permute-start.2 = (bf16[32,2,32,128]{3,1,0,2:T(2,128)(2,1)S(1)}, bf16[32,2,32,128]{3,1,0,2:T(2,128)(2,1)S(1)}, u32[]{:S(2)}, u32[]{:S(2)}) collective-permute-start(bf16[32,2,32,128]{3,1,0,2:T(2,128)(2,1)S(1)} %copy.8), channel_id=1, source_target_pairs={{12,0},{16,4},{20,8},{24,12},{28,16},{13,1},{17,5},{21,9},{25,13},... | collective-permute-start | bytes 1572872 | tf_op jit(solution)/shard_map/ppermute | solution.py:18
  28.6 27.2 %collective-permute-start.1 = (bf16[32,2,32,128]{3,1,0,2:T(2,128)(2,1)S(1)}, bf16[32,2,32,128]{3,1,0,2:T(2,128)(2,1)S(1)}, u32[]{:S(2)}, u32[]{:S(2)}) collective-permute-start(bf16[32,2,32,128]{3,1,0,2:T(2,128)(2,1)S(1)} %copy.8), channel_id=1, source_target_pairs={{8,0},{12,4},{16,8},{20,12},{24,16},{28,20},{9,1},{13,5},{17,9},{2... | collective-permute-start | bytes 1572872 | tf_op jit(solution)/shard_map/ppermute | solution.py:18
  29.9 25.4 %collective-permute-start = (bf16[32,2,32,128]{3,1,0,2:T(2,128)(2,1)S(1)}, bf16[32,2,32,128]{3,1,0,2:T(2,128)(2,1)S(1)}, u32[]{:S(2)}, u32[]{:S(2)}) collective-permute-start(bf16[32,2,32,128]{3,1,0,2:T(2,128)(2,1)S(1)} %copy.8), channel_id=1, source_target_pairs={{4,0},{8,4},{12,8},{16,12},{20,16},{24,20},{28,24},{5,1},{9,5},{13... | collective-permute-start | bytes 1572872 | tf_op jit(solution)/shard_map/ppermute | solution.py:18
  31.2 70.2 %collective-permute-start.3 = (bf16[32,2,32,128]{3,1,0,2:T(2,128)(2,1)S(1)}, bf16[32,2,32,128]{3,1,0,2:T(2,128)(2,1)S(1)}, u32[]{:S(2)}, u32[]{:S(2)}) collective-permute-start(bf16[32,2,32,128]{3,1,0,2:T(2,128)(2,1)S(1)} %copy.8), channel_id=1, source_target_pairs={{16,0},{20,4},{24,8},{28,12},{17,1},{21,5},{25,9},{29,13},{18,2},{... | collective-permute-start | bytes 1572872 | tf_op jit(solution)/shard_map/ppermute | solution.py:18
